TPU v7x, 32 devices: a whole 2x2x4 slice. The times are simulated.
32 devices in a mesh: blk: 8 (over z, y), grp: 4 (over x, core).
Axes of the slice: x: 2, y: 2, z: 4, core: 2. Of those that a mesh axis runs over, the one named last changes fastest.
Arguments:
- users: float32 [8192, 256], P(('blk', 'grp')), may hold values from -1.5 to 1.5
- items: float32 [8192, 256], P('blk'), may hold values from -1.5 to 1.5
- noise_users: float32 [2, 8192, 256], P(None, ('blk', 'grp')), may hold values from -6 to 6
- noise_items: float32 [2, 8192, 256], P(None, 'blk'), may hold values from -6 to 6
- tile_index: int32 [2, 256], P(None, ('blk', 'grp')), may hold values from 0 to 15, as said below
- counts: int32 [2, 32], P(None, ('blk', 'grp')), may hold values from 1 to 8, as said below
- ratings: bfloat16 [2, 256, 128, 128], P(None, ('blk', 'grp')), may hold values from -6 to 6
- weights: bfloat16 [2, 256, 128, 128], P(None, ('blk', 'grp')), may hold values from 0 to 2
Outputs:
- users_out: float32 [8192, 256], P(('blk', 'grp'))
- items_out: float32 [8192, 256], P(('blk', 'grp'))
Inputs may be any that keep to these rules, and one draw needn't show every extreme that they name: `tile_index`: slot t names user tile row t // 8 of the device's users and item tile column t % 8; the live slots of a device in a stratum name distinct tiles. `counts`: in every stratum some device has 8 live slots.
All inputs are finite; a program needn't handle non-finite values.
Results may differ from a plain program's by a relative error of at most 0.0003.
Values sent between devices are 32-bit elements; how exact they have to be, the bound alone decides.
A program may use at most 64 MiB of HBM per device.

v0:
```python
import functools
import math

import jax
import jax.numpy as jnp
from jax import lax
from jax.experimental import pallas as pl
from jax.experimental.pallas import tpu as pltpu
from jax.sharding import PartitionSpec as P

STEP_SIZE = 0.001
LIKELIHOOD = 20.0
NOISE_SCALE = math.sqrt(0.002)
TILE = 128
CHUNKS = 4
LAG = 2
MESH = pl.DeviceIdType.MESH
F32 = jnp.float32
BF16 = jnp.bfloat16

(S0_SIB_FAR, S0_X, S0_SIB_OWN, FORWARD, RELAY_SIB, RELAY_X, RELAY_LAST,
 S1_SIB_FAR, S1_X, S1_SIB_OWN, FINAL) = range(11)
KINDS = 11


def halves(value):
    high = value.astype(BF16)
    low = (value - high.astype(F32)).astype(BF16)
    return high, low


def dot3(left, right, contract):
    dims = (contract, ((), ()))
    dot = functools.partial(lax.dot_general, dimension_numbers=dims, preferred_element_type=F32)
    return dot(left[0], right[0]) + (dot(left[0], right[1]) + dot(left[1], right[0]))


def kernel(n_blk, tiles, counts, users_hbm, items_hbm, noise_users_hbm, noise_items_hbm,
           ratings_hbm, weights_hbm, users_out, items_out,
           users, items, position, noise_users, noise_items, ratings0, ratings1, weights0, weights1,
           u_high, u_low, v_high, v_low, e_high, e_low, part, from_sib_far, from_x,
           from_sib_own, moved, users_new, local_sem, out_sem, send_sem, recv_sem):
    quarter = users.shape[0]
    chunk = quarter // CHUNKS
    item_tiles = items.shape[0] // TILE
    slots = tiles.shape[1]
    blk = lax.axis_index("blk")
    grp = lax.axis_index("grp")
    side = grp // 2
    core = grp % 2
    sibling = (blk, side * 2 + (1 - core))
    across = (blk, (1 - side) * 2 + core)
    ahead = ((blk + 1) % n_blk, grp)
    behind = ((blk + n_blk - 1) % n_blk, grp)
    q_a = (1 - side) * 2 + core
    q_b = (1 - side) * 2 + (1 - core)
    q_c = side * 2 + core
    q_d = side * 2 + (1 - core)

    def rows(q, k=None):
        if k is None:
            return pl.ds(pl.multiple_of(q * quarter, quarter), quarter)
        return pl.ds(pl.multiple_of(q * quarter + k * chunk, chunk), chunk)

    def piece(k):
        return pl.ds(k * chunk, chunk)

    loads = [
        pltpu.make_async_copy(users_hbm, users, local_sem.at[0]),
        pltpu.make_async_copy(items_hbm, items, local_sem.at[1]),
        pltpu.make_async_copy(ratings_hbm.at[0], ratings0, local_sem.at[2]),
        pltpu.make_async_copy(weights_hbm.at[0], weights0, local_sem.at[3]),
        pltpu.make_async_copy(noise_items_hbm.at[0, rows(q_a)], noise_items.at[0], local_sem.at[4]),
        pltpu.make_async_copy(noise_users_hbm, noise_users, local_sem.at[5]),
        pltpu.make_async_copy(ratings_hbm.at[1], ratings1, local_sem.at[6]),
        pltpu.make_async_copy(weights_hbm.at[1], weights1, local_sem.at[7]),
        pltpu.make_async_copy(noise_items_hbm.at[1, rows(q_c)], noise_items.at[1], local_sem.at[8]),
    ]
    for load in loads:
        load.start()

    barrier = pltpu.get_barrier_semaphore()
    for other in (sibling, across, ahead, behind):
        pl.semaphore_signal(barrier, inc=1, device_id=other, device_id_type=MESH)

    def remote(kind, k, source, target, device):
        return pltpu.make_async_remote_copy(
            src_ref=source, dst_ref=target, send_sem=send_sem.at[kind, k],
            recv_sem=recv_sem.at[kind, k], device_id=device, device_id_type=MESH)

    def copy_of(kind, k):
        if kind in (S0_SIB_FAR, S1_SIB_FAR):
            s = 0 if kind == S0_SIB_FAR else 1
            return remote(kind, k, part.at[s, 0, piece(k)], from_sib_far.at[s, piece(k)], sibling)
        if kind in (S0_X, S1_X):
            s = 0 if kind == S0_X else 1
            return remote(kind, k, part.at[s, 1, piece(k)], from_x.at[s, piece(k)], across)
        if kind in (S0_SIB_OWN, S1_SIB_OWN):
            s = 0 if kind == S0_SIB_OWN else 1
            return remote(kind, k, part.at[s, 2, piece(k)], from_sib_own.at[s, piece(k)], sibling)
        if kind == FORWARD:
            return remote(kind, k, moved.at[0, piece(k)], position.at[rows(q_a, k)], ahead)
        if kind == RELAY_SIB:
            return remote(kind, k, position.at[rows(q_a, k)], position.at[rows(q_a, k)], sibling)
        if kind == RELAY_X:
            return remote(kind, k, position.at[rows(q_a, k)], position.at[rows(q_a, k)], across)
        if kind == RELAY_LAST:
            return remote(kind, k, position.at[rows(q_c, k)], position.at[rows(q_c, k)], sibling)
        return remote(kind, k, moved.at[1, piece(k)], items_out.at[piece(k)], ahead)

    def send(kind, k):
        copy_of(kind, k).start()

    def arrive(kind, k):
        copy_of(kind, k).wait_recv()

    def cell(stratum, row, column):
        wanted = row * item_tiles + column
        slot = jnp.int32(0)
        live = jnp.float32(0)
        for s in range(slots):
            hit = jnp.logical_and(tiles[stratum, s] == wanted, s < counts[0, stratum])
            slot = jnp.where(hit, s, slot)
            live = jnp.where(hit, jnp.float32(1), live)
        ratings, weights = ((ratings0, weights0), (ratings1, weights1))[stratum]
        return (ratings[slot].astype(F32), weights[slot].astype(F32) * live)

    def grads(stratum, place, q, block):
        user_parts = (u_high[...], u_low[...])
        v_high[place], v_low[place] = halves(block[rows(q), :])
        predicted = dot3(user_parts, (v_high[place], v_low[place]), ((1,), (1,)))
        bands = []
        for r in range(quarter // TILE):
            line = []
            for j in range(quarter // TILE):
                rating, weight = cell(stratum, r, q * (quarter // TILE) + j)
                line.append(weight * (rating - predicted[r * TILE:(r + 1) * TILE, j * TILE:(j + 1) * TILE]))
            bands.append(jnp.concatenate(line, axis=1))
        err = jnp.concatenate(bands, axis=0)
        e_high[place], e_low[place] = halves(err)
        return dot3(halves(err.T), user_parts, ((1,), (0,)))

    def user_step(stratum, now):
        total = jnp.zeros(now.shape, F32)
        for place in range(4):
            total += dot3((e_high[place], e_low[place]), (v_high[place], v_low[place]), ((1,), (0,)))
        return now + STEP_SIZE * (LIKELIHOOD * total - now) + NOISE_SCALE * noise_users[stratum]

    loads[0].wait()
    u_high[...], u_low[...] = halves(users[...])
    loads[1].wait()
    loads[2].wait()
    loads[3].wait()
    part[0, 0] = grads(0, 0, q_d, items)
    pl.semaphore_wait(barrier, 4)
    for k in range(CHUNKS):
        send(S0_SIB_FAR, k)
    part[0, 1] = grads(0, 1, q_c, items)
    for k in range(CHUNKS):
        arrive(S0_SIB_FAR, k)
        part[0, 1, piece(k)] += from_sib_far[0, piece(k)]
        send(S0_X, k)
    part[0, 2] = grads(0, 2, q_b, items)
    for k in range(CHUNKS):
        send(S0_SIB_OWN, k)
    part[0, 3] = grads(0, 3, q_a, items)
    loads[4].wait()
    loads[5].wait()
    users_new[...] = user_step(0, users[...])
    u_high[...], u_low[...] = halves(users_new[...])

    for k in range(CHUNKS + LAG):
        if k < CHUNKS:
            arrive(S0_SIB_OWN, k)
            arrive(S0_X, k)
            now = items[rows(q_a, k), :]
            total = part[0, 3, piece(k)] + from_sib_own[0, piece(k)] + from_x[0, piece(k)]
            moved[0, piece(k)] = (now + STEP_SIZE * (LIKELIHOOD * total - now)
                                  + NOISE_SCALE * noise_items[0, piece(k)])
            send(FORWARD, k)
        if k >= LAG:
            arrive(FORWARD, k - LAG)
            send(RELAY_X, k - LAG)
            send(RELAY_SIB, k - LAG)
    loads[6].wait()
    loads[7].wait()
    for k in range(CHUNKS):
        arrive(RELAY_SIB, k)
    part[1, 0] = grads(1, 0, q_b, position)
    for k in range(CHUNKS):
        send(S1_SIB_FAR, k)
    part[1, 1] = grads(1, 1, q_a, position)
    for k in range(CHUNKS):
        arrive(S1_SIB_FAR, k)
        part[1, 1, piece(k)] += from_sib_far[1, piece(k)]
        send(S1_X, k)
    for k in range(CHUNKS):
        arrive(RELAY_X, k)
        send(RELAY_LAST, k)
    part[1, 3] = grads(1, 3, q_c, position)
    for k in range(CHUNKS):
        arrive(RELAY_LAST, k)
    part[1, 2] = grads(1, 2, q_d, position)
    for k in range(CHUNKS):
        send(S1_SIB_OWN, k)
    users_new[...] = user_step(1, users_new[...])
    store = pltpu.make_async_copy(users_new, users_out, out_sem)
    store.start()
    loads[8].wait()
    for k in range(CHUNKS):
        arrive(S1_SIB_OWN, k)
        arrive(S1_X, k)
        now = position[rows(q_c, k), :]
        total = part[1, 3, piece(k)] + from_sib_own[1, piece(k)] + from_x[1, piece(k)]
        moved[1, piece(k)] = (now + STEP_SIZE * (LIKELIHOOD * total - now)
                              + NOISE_SCALE * noise_items[1, piece(k)])
        send(FINAL, k)
    for kind in range(KINDS):
        for k in range(CHUNKS):
            copy_of(kind, k).wait_send()
    store.wait()
    for k in range(CHUNKS):
        arrive(FINAL, k)


def body(n_blk, users, items, noise_users, noise_items, tile_index, counts, ratings, weights):
    mine, rank = users.shape
    slots, tile = ratings.shape[1], ratings.shape[2]
    square = (mine, mine)
    kept = (mine, rank)
    any_spec = pl.BlockSpec(memory_space=pl.ANY)
    smem_spec = pl.BlockSpec(memory_space=pltpu.SMEM)
    work = 2 * 3 * 3 * 2 * mine * items.shape[0] * rank
    return pl.pallas_call(
        functools.partial(kernel, n_blk),
        out_shape=(pltpu.VMEM(kept, F32), pltpu.VMEM(kept, F32)),
        in_specs=[smem_spec, smem_spec] + [any_spec] * 6,
        out_specs=(any_spec, any_spec),
        scratch_shapes=[
            pltpu.VMEM(kept, F32),
            pltpu.VMEM(items.shape, F32),
            pltpu.VMEM(items.shape, F32),
            pltpu.VMEM((2,) + kept, F32),
            pltpu.VMEM((2,) + kept, F32),
            pltpu.VMEM((slots, tile, tile), BF16),
            pltpu.VMEM((slots, tile, tile), BF16),
            pltpu.VMEM((slots, tile, tile), BF16),
            pltpu.VMEM((slots, tile, tile), BF16),
            pltpu.VMEM(kept, BF16),
            pltpu.VMEM(kept, BF16),
            pltpu.VMEM((4,) + kept, BF16),
            pltpu.VMEM((4,) + kept, BF16),
            pltpu.VMEM((4,) + square, BF16),
            pltpu.VMEM((4,) + square, BF16),
            pltpu.VMEM((2, 4) + kept, F32),
            pltpu.VMEM((2,) + kept, F32),
            pltpu.VMEM((2,) + kept, F32),
            pltpu.VMEM((2,) + kept, F32),
            pltpu.VMEM((2,) + kept, F32),
            pltpu.VMEM(kept, F32),
            pltpu.SemaphoreType.DMA((9,)),
            pltpu.SemaphoreType.DMA,
            pltpu.SemaphoreType.DMA((KINDS, CHUNKS)),
            pltpu.SemaphoreType.DMA((KINDS, CHUNKS)),
        ],
        compiler_params=pltpu.CompilerParams(
            collective_id=0, has_side_effects=True, vmem_limit_bytes=56 * 1024 * 1024),
        cost_estimate=pl.CostEstimate(flops=work, bytes_accessed=4 * 2 ** 20, transcendentals=0),
    )(tile_index, counts.T, users, items, noise_users, noise_items, ratings, weights)


def solution(mesh):
    in_specs = (
        P(("blk", "grp"), None),
        P("blk", None),
        P(None, ("blk", "grp"), None),
        P(None, "blk", None),
        P(None, ("blk", "grp")),
        P(None, ("blk", "grp")),
        P(None, ("blk", "grp"), None, None),
        P(None, ("blk", "grp"), None, None),
    )
    out_specs = (P(("blk", "grp"), None), P(("blk", "grp"), None))
    return jax.shard_map(functools.partial(body, mesh.shape["blk"]), mesh=mesh,
                         in_specs=in_specs, out_specs=out_specs, check_vma=False)
```

profile of v0, /device:TPU:0, one launch (start us, length us, event | category | flops | bytes accessed | tf_op | source)
XLA Modules:
  0.0 36.5 jit_solution(3037137413503397889)
XLA Ops:
  0.6 34.4 %shard_map.95 = (f32[256,256]{1,0:T(8,128)S(1)}, f32[256,256]{1,0:T(8,128)S(1)}) custom-call(s32[2,8]{1,0:T(2,128)} %tiles.1, s32[1,2]{1,0:T(1,128)} %bitcast.1, f32[256,256]{1,0:T(8,128)} %users_hbm.1, f32[1024,256]{1,0:T(8,128)} %items_hbm.1, f32[2,256,256]{2,1,0:T(8,128)} %noise_users_hbm.1, f32[2,1024,256]{2,1,0:T(8,128)} %noise_items_hbm.1, ...), custom_call_target="tpu_custom_call" | custom-call | flops 2415919104 | bytes 4194304 | tf_op jit(solution)/shard_map/pallas_call | solution.py:234
  35.1 0.7 %copy.12 = f32[256,256]{1,0:T(8,128)} copy(f32[256,256]{1,0:T(8,128)S(1)} %get-tuple-element.2) | data formatting | bytes 524288
  35.8 0.7 %copy.13 = f32[256,256]{1,0:T(8,128)} copy(f32[256,256]{1,0:T(8,128)S(1)} %get-tuple-element.3) | data formatting | bytes 524288
where the time goes:
time: 36.6 us; the launch traced here: 36.5 us
  Pallas kernels  34.4 us (94%)
  local copies, waits for them, and re-layouts  1.41 us (4%)
  between operations  0.64 us (2%)
    pallas_call x1, Pallas kernels, body(): pl.pallas_call(functools.partial(kernel, n_blk), out_shape=(pltpu.VMEM(ke...  34.4 us
    unnamed x2, local copies, waits for them, and re-layouts  1.41 us

commit v1 on v0

v1 whole, which is shorter than its diff:
```python
import functools
import math

import jax
import jax.numpy as jnp
from jax import lax
from jax.experimental import pallas as pl
from jax.experimental.pallas import tpu as pltpu
from jax.sharding import PartitionSpec as P

STEP_SIZE = 0.001
LIKELIHOOD = 20.0
NOISE_SCALE = math.sqrt(0.002)
TILE = 128
FINE = 4
MESH = pl.DeviceIdType.MESH
F32 = jnp.float32
BF16 = jnp.bfloat16

(S0_SIB_FAR, S0_X, S0_SIB_OWN, FORWARD, RELAY_SIB, RELAY_X, RELAY_LAST,
 S1_SIB_FAR, S1_X, S1_SIB_OWN, FINAL) = range(11)
KINDS = 11
ON_CHIP = (S0_SIB_FAR, S0_SIB_OWN, RELAY_SIB, RELAY_LAST, S1_SIB_FAR, S1_SIB_OWN)


def halves(value):
    high = value.astype(BF16)
    low = (value - high.astype(F32)).astype(BF16)
    return high, low


def dot3(left, right, contract):
    dims = (contract, ((), ()))
    dot = functools.partial(lax.dot_general, dimension_numbers=dims, preferred_element_type=F32)
    return dot(left[0], right[0]) + (dot(left[0], right[1]) + dot(left[1], right[0]))


def kernel(n_blk, tiles_hbm, counts_hbm, users_hbm, items_hbm, noise_users_hbm, noise_items_hbm,
           ratings_hbm, weights_hbm, users_out, items_out,
           tiles, counts, users, items, position, noise_users, noise_items, ratings0, ratings1, weights0, weights1,
           u_high, u_low, v_high, v_low, e_high, e_low, part, from_sib_far, from_x,
           from_sib_own, moved, users_new, local_sem, out_sem, send_sem, recv_sem):
    quarter = users.shape[0]
    per = quarter // TILE
    item_tiles = items.shape[0] // TILE
    slots = tiles.shape[1]
    blk = lax.axis_index("blk")
    grp = lax.axis_index("grp")
    side = grp // 2
    core = grp % 2
    sibling = (blk, side * 2 + (1 - core))
    across = (blk, (1 - side) * 2 + core)
    ahead = ((blk + 1) % n_blk, grp)
    behind = ((blk + n_blk - 1) % n_blk, grp)
    q_a = (1 - side) * 2 + core
    q_b = (1 - side) * 2 + (1 - core)
    q_c = side * 2 + core
    q_d = side * 2 + (1 - core)

    def rows(q, start=0, size=quarter):
        return pl.ds(pl.multiple_of(q * quarter + start, size), size)

    def chunk(kind):
        return TILE if kind in ON_CHIP else quarter // FINE

    def count(kind):
        return quarter // chunk(kind)

    def load(index, source, target):
        copy = pltpu.make_async_copy(source, target, local_sem.at[index])
        copy.start()
        return copy

    load_tiles = load(0, tiles_hbm, tiles)
    load_counts = load(1, counts_hbm, counts)
    load_users = load(2, users_hbm, users)
    load_items = [load(3, items_hbm.at[rows(q_d)], items.at[rows(q_d)])]
    load_ratings = [load(4, ratings_hbm.at[0], ratings0)]
    load_weights = [load(5, weights_hbm.at[0], weights0)]
    barrier = pltpu.get_barrier_semaphore()
    for other in (sibling, across, ahead, behind):
        pl.semaphore_signal(barrier, inc=1, device_id=other, device_id_type=MESH)
    for index, q in ((6, q_c), (7, q_b), (8, q_a)):
        load_items.append(load(index, items_hbm.at[rows(q)], items.at[rows(q)]))
    load_noise_users = load(9, noise_users_hbm, noise_users)
    load_noise_items = [load(10, noise_items_hbm.at[0, rows(q_a)], noise_items.at[0]),
                        load(11, noise_items_hbm.at[1, rows(q_c)], noise_items.at[1])]
    load_ratings.append(load(12, ratings_hbm.at[1], ratings1))
    load_weights.append(load(13, weights_hbm.at[1], weights1))

    def remote(kind, k, source, target, device):
        return pltpu.make_async_remote_copy(
            src_ref=source, dst_ref=target, send_sem=send_sem.at[kind, k],
            recv_sem=recv_sem.at[kind, k], device_id=device, device_id_type=MESH)

    def copy_of(kind, k):
        size = chunk(kind)
        piece = pl.ds(k * size, size)
        s = 0 if kind < S1_SIB_FAR else 1
        if kind in (S0_SIB_FAR, S1_SIB_FAR):
            return remote(kind, k, part.at[s, 0, piece], from_sib_far.at[s, piece], sibling)
        if kind in (S0_X, S1_X):
            return remote(kind, k, part.at[s, 1, piece], from_x.at[s, piece], across)
        if kind in (S0_SIB_OWN, S1_SIB_OWN):
            return remote(kind, k, part.at[s, 2, piece], from_sib_own.at[s, piece], sibling)
        if kind == FORWARD:
            return remote(kind, k, moved.at[0, piece], position.at[rows(q_a, k * size, size)], ahead)
        if kind == FINAL:
            return remote(kind, k, moved.at[1, piece], items_out.at[piece], ahead)
        where = rows(q_c if kind == RELAY_LAST else q_a, k * size, size)
        other = across if kind == RELAY_X else sibling
        return remote(kind, k, position.at[where], position.at[where], other)

    def send(kind, k):
        copy_of(kind, k).start()

    def arrive(kind, k):
        copy_of(kind, k).wait_recv()

    def cell(stratum, row, column):
        wanted = row * item_tiles + column
        slot = jnp.int32(0)
        live = jnp.float32(0)
        for s in range(slots):
            hit = jnp.logical_and(tiles[stratum, s] == wanted, s < counts[0, stratum])
            slot = jnp.where(hit, s, slot)
            live = jnp.where(hit, jnp.float32(1), live)
        ratings, weights = ((ratings0, weights0), (ratings1, weights1))[stratum]
        return (ratings[slot].astype(F32), weights[slot].astype(F32) * live)

    def grads(stratum, place, q, block, j):
        span = slice(j * TILE, (j + 1) * TILE)
        user_parts = (u_high[...], u_low[...])
        item_parts = halves(block[rows(q, j * TILE, TILE), :])
        v_high[place, span], v_low[place, span] = item_parts
        predicted = dot3(user_parts, item_parts, ((1,), (1,)))
        bands = []
        for r in range(per):
            rating, weight = cell(stratum, r, q * per + j)
            bands.append(weight * (rating - predicted[r * TILE:(r + 1) * TILE]))
        err = jnp.concatenate(bands, axis=0)
        e_high[place, :, span], e_low[place, :, span] = halves(err)
        part[stratum, place, span] = dot3(halves(err.T), user_parts, ((1,), (0,)))

    def send_far(stratum, j):
        span = slice(j * TILE, (j + 1) * TILE)
        arrive((S0_SIB_FAR, S1_SIB_FAR)[stratum], j)
        part[stratum, 1, span] += from_sib_far[stratum, span]
        kind = (S0_X, S1_X)[stratum]
        for k in range(j * FINE // per, (j + 1) * FINE // per):
            send(kind, k)

    def user_step(stratum, now):
        total = jnp.zeros(now.shape, F32)
        for place in range(4):
            total += dot3((e_high[place], e_low[place]), (v_high[place], v_low[place]), ((1,), (0,)))
        return now + STEP_SIZE * (LIKELIHOOD * total - now) + NOISE_SCALE * noise_users[stratum]

    def item_step(stratum, now, k):
        piece = pl.ds(k * quarter // FINE, quarter // FINE)
        arrive((S0_X, S1_X)[stratum], k)
        total = part[stratum, 3, piece] + from_sib_own[stratum, piece] + from_x[stratum, piece]
        moved[stratum, piece] = (now + STEP_SIZE * (LIKELIHOOD * total - now)
                                 + NOISE_SCALE * noise_items[stratum, piece])
        send((FORWARD, FINAL)[stratum], k)

    load_users.wait()
    u_high[...], u_low[...] = halves(users[...])
    load_tiles.wait()
    load_counts.wait()
    load_items[0].wait()
    load_ratings[0].wait()
    load_weights[0].wait()
    for j in range(per):
        grads(0, 0, q_d, items, j)
        if j == 0:
            pl.semaphore_wait(barrier, 4)
        send(S0_SIB_FAR, j)
    load_items[1].wait()
    for j in range(per):
        grads(0, 1, q_c, items, j)
        send_far(0, j)
    load_items[2].wait()
    for j in range(per):
        grads(0, 2, q_b, items, j)
        send(S0_SIB_OWN, j)
    load_items[3].wait()
    for j in range(per):
        grads(0, 3, q_a, items, j)
    load_noise_users.wait()
    users_new[...] = user_step(0, users[...])
    u_high[...], u_low[...] = halves(users_new[...])
    load_noise_items[0].wait()
    for load_late in (load_ratings[1], load_weights[1], load_noise_items[1]):
        load_late.wait()

    def relay(k):
        arrive(FORWARD, k)
        send(RELAY_X, k)
        if (k + 1) * per % FINE == 0:
            send(RELAY_SIB, (k + 1) * per // FINE - 1)

    fine = quarter // FINE
    for k in range(FINE):
        if k * per % FINE == 0:
            arrive(S0_SIB_OWN, k * per // FINE)
        item_step(0, items[rows(q_a, k * fine, fine), :], k)
        if k >= FINE - 2:
            relay(k - (FINE - 2))
    for j in range(per):
        arrive(RELAY_SIB, j)
        grads(1, 0, q_b, position, j)
        send(S1_SIB_FAR, j)
        if j == 0:
            relay(FINE - 2)
        grads(1, 1, q_a, position, j)
        send_far(1, j)
        if j == 0:
            relay(FINE - 1)
    for j in range(per):
        for k in range(j * FINE // per, (j + 1) * FINE // per):
            arrive(RELAY_X, k)
        send(RELAY_LAST, j)
        grads(1, 3, q_c, position, j)
    for j in range(per):
        arrive(RELAY_LAST, j)
        grads(1, 2, q_d, position, j)
        send(S1_SIB_OWN, j)
    users_new[...] = user_step(1, users_new[...])
    store = pltpu.make_async_copy(users_new, users_out, out_sem)
    store.start()
    for k in range(FINE):
        if k * per % FINE == 0:
            arrive(S1_SIB_OWN, k * per // FINE)
        item_step(1, position[rows(q_c, k * fine, fine), :], k)
    for kind in range(KINDS):
        for k in range(count(kind)):
            copy_of(kind, k).wait_send()
    store.wait()
    for k in range(FINE):
        arrive(FINAL, k)


def body(n_blk, users, items, noise_users, noise_items, tile_index, counts, ratings, weights):
    mine, rank = users.shape
    slots, tile = ratings.shape[1], ratings.shape[2]
    square = (mine, mine)
    kept = (mine, rank)
    any_spec = pl.BlockSpec(memory_space=pl.ANY)
    work = 2 * 3 * 3 * 2 * mine * items.shape[0] * rank
    return pl.pallas_call(
        functools.partial(kernel, n_blk),
        out_shape=(pltpu.VMEM(kept, F32), pltpu.VMEM(kept, F32)),
        in_specs=[any_spec] * 8,
        out_specs=(any_spec, any_spec),
        scratch_shapes=[
            pltpu.SMEM(tile_index.shape, jnp.int32),
            pltpu.SMEM((1, counts.shape[0]), jnp.int32),
            pltpu.VMEM(kept, F32),
            pltpu.VMEM(items.shape, F32),
            pltpu.VMEM(items.shape, F32),
            pltpu.VMEM((2,) + kept, F32),
            pltpu.VMEM((2,) + kept, F32),
            pltpu.VMEM((slots, tile, tile), BF16),
            pltpu.VMEM((slots, tile, tile), BF16),
            pltpu.VMEM((slots, tile, tile), BF16),
            pltpu.VMEM((slots, tile, tile), BF16),
            pltpu.VMEM(kept, BF16),
            pltpu.VMEM(kept, BF16),
            pltpu.VMEM((4,) + kept, BF16),
            pltpu.VMEM((4,) + kept, BF16),
            pltpu.VMEM((4,) + square, BF16),
            pltpu.VMEM((4,) + square, BF16),
            pltpu.VMEM((2, 4) + kept, F32),
            pltpu.VMEM((2,) + kept, F32),
            pltpu.VMEM((2,) + kept, F32),
            pltpu.VMEM((2,) + kept, F32),
            pltpu.VMEM((2,) + kept, F32),
            pltpu.VMEM(kept, F32),
            pltpu.SemaphoreType.DMA((14,)),
            pltpu.SemaphoreType.DMA,
            pltpu.SemaphoreType.DMA((KINDS, FINE)),
            pltpu.SemaphoreType.DMA((KINDS, FINE)),
        ],
        compiler_params=pltpu.CompilerParams(
            collective_id=0, has_side_effects=True, vmem_limit_bytes=56 * 1024 * 1024),
        cost_estimate=pl.CostEstimate(flops=work, bytes_accessed=4 * 2 ** 20, transcendentals=0),
    )(tile_index, counts.T, users, items, noise_users, noise_items, ratings, weights)


def solution(mesh):
    in_specs = (
        P(("blk", "grp"), None),
        P("blk", None),
        P(None, ("blk", "grp"), None),
        P(None, "blk", None),
        P(None, ("blk", "grp")),
        P(None, ("blk", "grp")),
        P(None, ("blk", "grp"), None, None),
        P(None, ("blk", "grp"), None, None),
    )
    out_specs = (P(("blk", "grp"), None), P(("blk", "grp"), None))
    return jax.shard_map(functools.partial(body, mesh.shape["blk"]), mesh=mesh,
                         in_specs=in_specs, out_specs=out_specs, check_vma=False)
```

time: 36.6 us -> 40.4 us (1.10)
  Pallas kernels: 34.4 us -> 38.2 us
    pallas_call x1, Pallas kernels: 34.4 us -> 38.2 us  [body(): pl.pallas_call(functools.partial(kernel, n_blk), out_shape=(pltpu.VMEM(ke...]
where the time goes in v1:
time: 40.4 us; the launch traced here: 40.3 us
  Pallas kernels  38.2 us (95%)
  local copies, waits for them, and re-layouts  1.41 us (3%)
  between operations  0.64 us (2%)
    pallas_call x1, Pallas kernels, body(): pl.pallas_call(functools.partial(kernel, n_blk), out_shape=(pltpu.VMEM(ke...  38.2 us
    unnamed x2, local copies, waits for them, and re-layouts  1.41 us

profile of v1, /device:TPU:0, one launch (start us, length us, event | category | flops | bytes accessed | tf_op | source)
XLA Modules:
  0.0 40.3 jit_solution(16459670574831236808)
XLA Ops:
  0.6 38.2 %shard_map.95 = (f32[256,256]{1,0:T(8,128)S(1)}, f32[256,256]{1,0:T(8,128)S(1)}) custom-call(s32[2,8]{1,0:T(2,128)} %tiles_hbm.1, s32[1,2]{1,0:T(1,128)} %bitcast.1, f32[256,256]{1,0:T(8,128)} %users_hbm.1, f32[1024,256]{1,0:T(8,128)} %items_hbm.1, f32[2,256,256]{2,1,0:T(8,128)} %noise_users_hbm.1, f32[2,1024,256]{2,1,0:T(8,128)} %noise_items_hbm.1, ...), custom_call_target="tpu_custom_call" | custom-call | flops 2415919104 | bytes 4194304 | tf_op jit(solution)/shard_map/pallas_call | solution.py:251
  38.9 0.7 %copy.12 = f32[256,256]{1,0:T(8,128)} copy(f32[256,256]{1,0:T(8,128)S(1)} %get-tuple-element.2) | data formatting | bytes 524288
  39.6 0.7 %copy.13 = f32[256,256]{1,0:T(8,128)} copy(f32[256,256]{1,0:T(8,128)S(1)} %get-tuple-element.3) | data formatting | bytes 524288

commit v2 on v1

v2 whole, which is shorter than its diff:
```python
import functools
import math

import jax
import jax.numpy as jnp
from jax import lax
from jax.experimental import pallas as pl
from jax.experimental.pallas import tpu as pltpu
from jax.sharding import PartitionSpec as P

STEP_SIZE = 0.001
LIKELIHOOD = 20.0
NOISE_SCALE = math.sqrt(0.002)
TILE = 128
FINE = 4
MESH = pl.DeviceIdType.MESH
F32 = jnp.float32
BF16 = jnp.bfloat16

(S0_SIB_FAR, S0_X, S0_SIB_OWN, FORWARD, RELAY_SIB, RELAY_X, RELAY_LAST,
 S1_SIB_FAR, S1_X, S1_SIB_OWN, FINAL) = range(11)
KINDS = 11
ON_CHIP = (S0_SIB_FAR, S0_SIB_OWN, RELAY_SIB, RELAY_LAST, S1_SIB_FAR, S1_SIB_OWN)


def halves(value):
    high = value.astype(BF16)
    low = (value - high.astype(F32)).astype(BF16)
    return high, low


def dot(left, right, contract):
    return lax.dot_general(left, right, (contract, ((), ())), preferred_element_type=F32)


def left_triple(value, axis):
    high, low = halves(value)
    return jnp.concatenate([high, low, high], axis=axis)


def right_triple(value, axis):
    high, low = halves(value)
    return jnp.concatenate([high, high, low], axis=axis)


def kernel(n_blk, tiles_hbm, counts_hbm, users_hbm, items_hbm, noise_users_hbm, noise_items_hbm,
           ratings_hbm, weights_hbm, users_out, items_out,
           tiles, counts, users, blocks, noise_users, noise_items, ratings, weights,
           u_wide, u_tall, v_tall, e_wide, part, from_sib_far, from_x,
           from_sib_own, moved, local_sem, out_sem, send_sem, recv_sem):
    quarter = users.shape[0]
    per = quarter // TILE
    items = blocks.at[0]
    position = blocks.at[1]
    item_tiles = items.shape[0] // TILE
    slots = tiles.shape[1]
    blk = lax.axis_index("blk")
    grp = lax.axis_index("grp")
    side = grp // 2
    core = grp % 2
    sibling = (blk, side * 2 + (1 - core))
    across = (blk, (1 - side) * 2 + core)
    ahead = ((blk + 1) % n_blk, grp)
    behind = ((blk + n_blk - 1) % n_blk, grp)
    q_a = (1 - side) * 2 + core
    q_b = (1 - side) * 2 + (1 - core)
    q_c = side * 2 + core
    q_d = side * 2 + (1 - core)

    def rows(q, start=0, size=quarter):
        return pl.ds(pl.multiple_of(q * quarter + start, size), size)

    def chunk(kind):
        return TILE if kind in ON_CHIP else quarter // FINE

    def count(kind):
        return quarter // chunk(kind)

    def load(index, source, target):
        copy = pltpu.make_async_copy(source, target, local_sem.at[index])
        copy.start()
        return copy

    load_tiles = load(0, tiles_hbm, tiles)
    load_counts = load(1, counts_hbm, counts)
    load_users = load(2, users_hbm, users)
    load_items = [load(3, items_hbm.at[rows(q_d)], items.at[rows(q_d)])]
    load_ratings = load(4, ratings_hbm, ratings)
    load_weights = load(5, weights_hbm, weights)
    barrier = pltpu.get_barrier_semaphore()
    for other in (sibling, across, ahead, behind):
        pl.semaphore_signal(barrier, inc=1, device_id=other, device_id_type=MESH)
    for index, q in ((6, q_c), (7, q_b), (8, q_a)):
        load_items.append(load(index, items_hbm.at[rows(q)], items.at[rows(q)]))
    load_noise_users = load(9, noise_users_hbm, noise_users)
    load_noise_items = [load(10, noise_items_hbm.at[0, rows(q_a)], noise_items.at[0]),
                        load(11, noise_items_hbm.at[1, rows(q_c)], noise_items.at[1])]

    def remote(kind, k, source, target, device):
        return pltpu.make_async_remote_copy(
            src_ref=source, dst_ref=target, send_sem=send_sem.at[kind, k],
            recv_sem=recv_sem.at[kind, k], device_id=device, device_id_type=MESH)

    def copy_of(kind, k):
        size = chunk(kind)
        piece = pl.ds(k * size, size)
        s = 0 if kind < S1_SIB_FAR else 1
        if kind in (S0_SIB_FAR, S1_SIB_FAR):
            return remote(kind, k, part.at[s, 0, piece], from_sib_far.at[s, piece], sibling)
        if kind in (S0_X, S1_X):
            return remote(kind, k, part.at[s, 1, piece], from_x.at[s, piece], across)
        if kind in (S0_SIB_OWN, S1_SIB_OWN):
            return remote(kind, k, part.at[s, 2, piece], from_sib_own.at[s, piece], sibling)
        if kind == FORWARD:
            return remote(kind, k, moved.at[0, piece], position.at[rows(q_a, k * size, size)], ahead)
        if kind == FINAL:
            return remote(kind, k, moved.at[1, piece], items_out.at[piece], ahead)
        where = rows(q_c if kind == RELAY_LAST else q_a, k * size, size)
        other = across if kind == RELAY_X else sibling
        return remote(kind, k, position.at[where], position.at[where], other)

    def send(kind, k):
        copy_of(kind, k).start()

    def arrive(kind, k):
        copy_of(kind, k).wait_recv()

    def cell(stratum, row, column):
        wanted = row * item_tiles + column
        slot = jnp.int32(0)
        live = jnp.float32(0)
        for s in range(slots):
            hit = jnp.logical_and(tiles[stratum, s] == wanted, s < counts[0, stratum])
            slot = jnp.where(hit, s, slot)
            live = jnp.where(hit, jnp.float32(1), live)
        return (ratings[stratum, slot].astype(F32), weights[stratum, slot].astype(F32) * live)

    def grads(stratum, place, q, target):
        item_rows = blocks[stratum, rows(q), :]
        predicted = dot(u_wide[...], right_triple(item_rows, 1), ((1,), (1,)))
        v_tall[place] = right_triple(item_rows, 0)
        bands = []
        for r in range(per):
            line = []
            for j in range(per):
                rating, weight = cell(stratum, r, q * per + j)
                line.append(weight * (rating - predicted[r * TILE:(r + 1) * TILE, j * TILE:(j + 1) * TILE]))
            bands.append(jnp.concatenate(line, axis=1))
        err = jnp.concatenate(bands, axis=0)
        e_wide[place] = left_triple(err, 1)
        part[stratum, target] = dot(left_triple(err.T, 1), u_tall[...], ((1,), (0,)))

    def send_far(stratum, j):
        span = slice(j * TILE, (j + 1) * TILE)
        arrive((S0_SIB_FAR, S1_SIB_FAR)[stratum], j)
        part[stratum, 1, span] += from_sib_far[stratum, span]
        kind = (S0_X, S1_X)[stratum]
        for k in range(j * FINE // per, (j + 1) * FINE // per):
            send(kind, k)

    def split_users():
        now = users[...]
        u_wide[...] = left_triple(now, 1)
        u_tall[...] = right_triple(now, 0)

    def user_step(stratum):
        now = users[...]
        total = dot(jnp.concatenate([e_wide[p] for p in range(4)], axis=1),
                    jnp.concatenate([v_tall[p] for p in range(4)], axis=0), ((1,), (0,)))
        users[...] = now + STEP_SIZE * (LIKELIHOOD * total - now) + NOISE_SCALE * noise_users[stratum]

    def item_step(stratum, now, k):
        piece = pl.ds(k * quarter // FINE, quarter // FINE)
        arrive((S0_X, S1_X)[stratum], k)
        total = part[stratum, 3, piece] + from_sib_own[stratum, piece] + from_x[stratum, piece]
        moved[stratum, piece] = (now + STEP_SIZE * (LIKELIHOOD * total - now)
                                 + NOISE_SCALE * noise_items[stratum, piece])
        send((FORWARD, FINAL)[stratum], k)

    def relay(k):
        arrive(FORWARD, k)
        send(RELAY_X, k)
        if (k + 1) * per % FINE == 0:
            send(RELAY_SIB, (k + 1) * per // FINE - 1)

    def finish(stratum, q):
        fine = quarter // FINE
        for k in range(FINE):
            if k * per % FINE == 0:
                arrive((S0_SIB_OWN, S1_SIB_OWN)[stratum], k * per // FINE)
            item_step(stratum, blocks[stratum, rows(q, k * fine, fine), :], k)
            if stratum == 0 and k >= 2:
                relay(k - 2)

    def send_all(kind):
        for j in range(count(kind)):
            send(kind, j)

    def arrive_all(kind):
        for j in range(count(kind)):
            arrive(kind, j)

    load_users.wait()
    split_users()
    load_tiles.wait()
    load_counts.wait()
    load_ratings.wait()
    load_weights.wait()
    pl.semaphore_wait(barrier, 4)

    def step(i, carry):
        stratum = i // 4
        place = i % 4
        q = jnp.where(jnp.logical_or(i == 0, i == 7), q_d,
                      jnp.where(jnp.logical_or(i == 1, i == 6), q_c,
                                jnp.where(jnp.logical_or(i == 2, i == 4), q_b, q_a)))
        target = jnp.where(i < 6, place, 9 - i)
        for p in range(4):
            @pl.when(i == p)
            def _():
                load_items[p].wait()

        @pl.when(i == 4)
        def _():
            for k in range(FINE - 2, FINE):
                relay(k)
            arrive_all(RELAY_SIB)

        @pl.when(i == 6)
        def _():
            arrive_all(RELAY_X)
            send_all(RELAY_LAST)

        @pl.when(i == 7)
        def _():
            arrive_all(RELAY_LAST)

        grads(stratum, place, q, target)

        @pl.when(i == 0)
        def _():
            send_all(S0_SIB_FAR)

        @pl.when(i == 1)
        def _():
            for j in range(per):
                send_far(0, j)

        @pl.when(i == 2)
        def _():
            send_all(S0_SIB_OWN)

        @pl.when(i == 4)
        def _():
            send_all(S1_SIB_FAR)

        @pl.when(i == 5)
        def _():
            for j in range(per):
                send_far(1, j)

        @pl.when(i == 7)
        def _():
            send_all(S1_SIB_OWN)

        @pl.when(i == 3)
        def _():
            load_noise_users.wait()

        @pl.when(place == 3)
        def _():
            user_step(stratum)

        @pl.when(i == 3)
        def _():
            split_users()
            for late in load_noise_items:
                late.wait()
            finish(0, q_a)

        return carry

    lax.fori_loop(0, 8, step, 0)
    store = pltpu.make_async_copy(users, users_out, out_sem)
    store.start()
    finish(1, q_c)
    for kind in range(KINDS):
        for k in range(count(kind)):
            copy_of(kind, k).wait_send()
    store.wait()
    arrive_all(FINAL)


def body(n_blk, users, items, noise_users, noise_items, tile_index, counts, ratings, weights):
    mine, rank = users.shape
    slots, tile = ratings.shape[1], ratings.shape[2]
    kept = (mine, rank)
    any_spec = pl.BlockSpec(memory_space=pl.ANY)
    work = 2 * 3 * 3 * 2 * mine * items.shape[0] * rank
    return pl.pallas_call(
        functools.partial(kernel, n_blk),
        out_shape=(pltpu.VMEM(kept, F32), pltpu.VMEM(kept, F32)),
        in_specs=[any_spec] * 8,
        out_specs=(any_spec, any_spec),
        scratch_shapes=[
            pltpu.SMEM(tile_index.shape, jnp.int32),
            pltpu.SMEM((1, counts.shape[0]), jnp.int32),
            pltpu.VMEM(kept, F32),
            pltpu.VMEM((2,) + items.shape, F32),
            pltpu.VMEM((2,) + kept, F32),
            pltpu.VMEM((2,) + kept, F32),
            pltpu.VMEM((2, slots, tile, tile), BF16),
            pltpu.VMEM((2, slots, tile, tile), BF16),
            pltpu.VMEM((mine, 3 * rank), BF16),
            pltpu.VMEM((3 * mine, rank), BF16),
            pltpu.VMEM((4, 3 * mine, rank), BF16),
            pltpu.VMEM((4, mine, 3 * mine), BF16),
            pltpu.VMEM((2, 4) + kept, F32),
            pltpu.VMEM((2,) + kept, F32),
            pltpu.VMEM((2,) + kept, F32),
            pltpu.VMEM((2,) + kept, F32),
            pltpu.VMEM((2,) + kept, F32),
            pltpu.SemaphoreType.DMA((12,)),
            pltpu.SemaphoreType.DMA,
            pltpu.SemaphoreType.DMA((KINDS, FINE)),
            pltpu.SemaphoreType.DMA((KINDS, FINE)),
        ],
        compiler_params=pltpu.CompilerParams(
            collective_id=0, has_side_effects=True, vmem_limit_bytes=56 * 1024 * 1024),
        cost_estimate=pl.CostEstimate(flops=work, bytes_accessed=4 * 2 ** 20, transcendentals=0),
    )(tile_index, counts.T, users, items, noise_users, noise_items, ratings, weights)


def solution(mesh):
    in_specs = (
        P(("blk", "grp"), None),
        P("blk", None),
        P(None, ("blk", "grp"), None),
        P(None, "blk", None),
        P(None, ("blk", "grp")),
        P(None, ("blk", "grp")),
        P(None, ("blk", "grp"), None, None),
        P(None, ("blk", "grp"), None, None),
    )
    out_specs = (P(("blk", "grp"), None), P(("blk", "grp"), None))
    return jax.shard_map(functools.partial(body, mesh.shape["blk"]), mesh=mesh,
                         in_specs=in_specs, out_specs=out_specs, check_vma=False)
```

time: 40.4 us -> 36.3 us (0.90)
  Pallas kernels: 38.2 us -> 34.1 us
    pallas_call x1, Pallas kernels: 38.2 us -> 34.1 us  [body(): pl.pallas_call(functools.partial(kernel, n_blk), out_shape=(pltpu.VMEM(ke...]
where the time goes in v2:
time: 36.3 us; the launch traced here: 36.2 us
  Pallas kernels  34.1 us (94%)
  local copies, waits for them, and re-layouts  1.41 us (4%)
  between operations  0.64 us (2%)
    pallas_call x1, Pallas kernels, body(): pl.pallas_call(functools.partial(kernel, n_blk), out_shape=(pltpu.VMEM(ke...  34.1 us
    unnamed x2, local copies, waits for them, and re-layouts  1.41 us

profile of v2, /device:TPU:0, one launch (start us, length us, event | category | flops | bytes accessed | tf_op | source)
XLA Modules:
  0.0 36.2 jit_solution(14162088733889981696)
XLA Ops:
  0.6 34.1 %shard_map.95 = (f32[256,256]{1,0:T(8,128)S(1)}, f32[256,256]{1,0:T(8,128)S(1)}) custom-call(s32[2,8]{1,0:T(2,128)} %tiles_hbm.1, s32[1,2]{1,0:T(1,128)} %bitcast.1, f32[256,256]{1,0:T(8,128)} %users_hbm.1, f32[1024,256]{1,0:T(8,128)} %items_hbm.1, f32[2,256,256]{2,1,0:T(8,128)} %noise_users_hbm.1, f32[2,1024,256]{2,1,0:T(8,128)} %noise_items_hbm.1, ...), custom_call_target="tpu_custom_call" | custom-call | flops 2415919104 | bytes 4194304 | tf_op jit(solution)/shard_map/pallas_call | solution.py:300
  34.8 0.7 %copy.12 = f32[256,256]{1,0:T(8,128)} copy(f32[256,256]{1,0:T(8,128)S(1)} %get-tuple-element.2) | data formatting | bytes 524288
  35.5 0.7 %copy.13 = f32[256,256]{1,0:T(8,128)} copy(f32[256,256]{1,0:T(8,128)S(1)} %get-tuple-element.3) | data formatting | bytes 524288

commit v3 on v2

--- a/solution.py
+++ b/solution.py
@@ -45,7 +45,7 @@
 
 def kernel(n_blk, tiles_hbm, counts_hbm, users_hbm, items_hbm, noise_users_hbm, noise_items_hbm,
            ratings_hbm, weights_hbm, users_out, items_out,
-           tiles, counts, users, blocks, noise_users, noise_items, ratings, weights,
+           tiles, counts, table, users, blocks, noise_users, noise_items, ratings, weights,
            u_wide, u_tall, v_tall, e_wide, part, from_sib_far, from_x,
            from_sib_own, moved, local_sem, out_sem, send_sem, recv_sem):
     quarter = users.shape[0]
@@ -125,30 +125,43 @@
     def arrive(kind, k):
         copy_of(kind, k).wait_recv()
 
-    def cell(stratum, row, column):
-        wanted = row * item_tiles + column
-        slot = jnp.int32(0)
-        live = jnp.float32(0)
+    def fill_table(i, carry):
+        stratum = i // (per * item_tiles)
+        wanted = i % (per * item_tiles)
+        slot = jnp.int32(-1)
         for s in range(slots):
             hit = jnp.logical_and(tiles[stratum, s] == wanted, s < counts[0, stratum])
             slot = jnp.where(hit, s, slot)
-            live = jnp.where(hit, jnp.float32(1), live)
-        return (ratings[stratum, slot].astype(F32), weights[stratum, slot].astype(F32) * live)
-
-    def grads(stratum, place, q, target):
-        item_rows = blocks[stratum, rows(q), :]
+        table[i] = slot
+        return carry
+
+    def cell_err(stratum, row, column, predicted):
+        slot = table[(stratum * per + row) * item_tiles + column]
+        live = jnp.where(slot >= 0, jnp.float32(1), jnp.float32(0))
+        slot = jnp.maximum(slot, 0)
+        weight = weights[stratum, slot].astype(F32) * live
+        return weight * (ratings[stratum, slot].astype(F32) - predicted)
+
+    def grads(stratum, place, q, start, size):
+        item_rows = blocks[stratum, rows(q, start, size), :]
         predicted = dot(u_wide[...], right_triple(item_rows, 1), ((1,), (1,)))
-        v_tall[place] = right_triple(item_rows, 0)
         bands = []
         for r in range(per):
             line = []
-            for j in range(per):
-                rating, weight = cell(stratum, r, q * per + j)
-                line.append(weight * (rating - predicted[r * TILE:(r + 1) * TILE, j * TILE:(j + 1) * TILE]))
+            for j in range(size // TILE):
+                column = q * per + start // TILE + j
+                line.append(cell_err(stratum, r, column,
+                                     predicted[r * TILE:(r + 1) * TILE, j * TILE:(j + 1) * TILE]))
             bands.append(jnp.concatenate(line, axis=1))
         err = jnp.concatenate(bands, axis=0)
-        e_wide[place] = left_triple(err, 1)
-        part[stratum, target] = dot(left_triple(err.T, 1), u_tall[...], ((1,), (0,)))
+        part[stratum, place, pl.ds(start, size)] = dot(left_triple(err.T, 1), u_tall[...], ((1,), (0,)))
+        item_high, item_low = halves(item_rows)
+        err_high, err_low = halves(err)
+        for third, item_part, err_part in ((0, item_high, err_high), (1, item_high, err_low),
+                                           (2, item_low, err_high)):
+            span = pl.ds(pl.multiple_of(third * quarter + start, size), size)
+            v_tall[place, span] = item_part
+            e_wide[place, :, span] = err_part
 
     def send_far(stratum, j):
         span = slice(j * TILE, (j + 1) * TILE)
@@ -183,14 +196,11 @@
         if (k + 1) * per % FINE == 0:
             send(RELAY_SIB, (k + 1) * per // FINE - 1)
 
-    def finish(stratum, q):
+    def finish(stratum, q, k):
         fine = quarter // FINE
-        for k in range(FINE):
-            if k * per % FINE == 0:
-                arrive((S0_SIB_OWN, S1_SIB_OWN)[stratum], k * per // FINE)
-            item_step(stratum, blocks[stratum, rows(q, k * fine, fine), :], k)
-            if stratum == 0 and k >= 2:
-                relay(k - 2)
+        if k * per % FINE == 0:
+            arrive((S0_SIB_OWN, S1_SIB_OWN)[stratum], k * per // FINE)
+        item_step(stratum, blocks[stratum, rows(q, k * fine, fine), :], k)
 
     def send_all(kind):
         for j in range(count(kind)):
@@ -200,42 +210,22 @@
         for j in range(count(kind)):
             arrive(kind, j)
 
+    load_tiles.wait()
+    load_counts.wait()
+    lax.fori_loop(0, 2 * per * item_tiles, fill_table, 0)
     load_users.wait()
     split_users()
-    load_tiles.wait()
-    load_counts.wait()
     load_ratings.wait()
     load_weights.wait()
     pl.semaphore_wait(barrier, 4)
 
-    def step(i, carry):
-        stratum = i // 4
-        place = i % 4
-        q = jnp.where(jnp.logical_or(i == 0, i == 7), q_d,
-                      jnp.where(jnp.logical_or(i == 1, i == 6), q_c,
-                                jnp.where(jnp.logical_or(i == 2, i == 4), q_b, q_a)))
-        target = jnp.where(i < 6, place, 9 - i)
+    def first(i, carry):
         for p in range(4):
             @pl.when(i == p)
             def _():
                 load_items[p].wait()
 
-        @pl.when(i == 4)
-        def _():
-            for k in range(FINE - 2, FINE):
-                relay(k)
-            arrive_all(RELAY_SIB)
-
-        @pl.when(i == 6)
-        def _():
-            arrive_all(RELAY_X)
-            send_all(RELAY_LAST)
-
-        @pl.when(i == 7)
-        def _():
-            arrive_all(RELAY_LAST)
-
-        grads(stratum, place, q, target)
+        grads(0, i, jnp.where(i == 0, q_d, jnp.where(i == 1, q_c, jnp.where(i == 2, q_b, q_a))), 0, quarter)
 
         @pl.when(i == 0)
         def _():
@@ -250,40 +240,66 @@
         def _():
             send_all(S0_SIB_OWN)
 
-        @pl.when(i == 4)
-        def _():
-            send_all(S1_SIB_FAR)
-
-        @pl.when(i == 5)
-        def _():
-            for j in range(per):
-                send_far(1, j)
-
-        @pl.when(i == 7)
-        def _():
-            send_all(S1_SIB_OWN)
-
-        @pl.when(i == 3)
-        def _():
-            load_noise_users.wait()
-
-        @pl.when(place == 3)
-        def _():
-            user_step(stratum)
-
-        @pl.when(i == 3)
-        def _():
-            split_users()
-            for late in load_noise_items:
-                late.wait()
-            finish(0, q_a)
-
         return carry
 
-    lax.fori_loop(0, 8, step, 0)
+    lax.fori_loop(0, 4, first, 0)
+    load_noise_items[0].wait()
+    finish(0, q_a, 0)
+    load_noise_users.wait()
+    user_step(0)
+    split_users()
+    for k in range(1, FINE):
+        finish(0, q_a, k)
+        if k >= 2:
+            relay(k - 2)
+
+    def second(i, carry):
+        place = jnp.where(i < 4, i % 2, 3 - (i - 4) // 2)
+        j = jnp.where(i < 4, i // 2, i % 2)
+        q = jnp.where(place == 0, q_b, jnp.where(place == 1, q_a, jnp.where(place == 2, q_d, q_c)))
+        for n in range(per):
+            @pl.when(i == 2 * n)
+            def _():
+                arrive(RELAY_SIB, n)
+
+            @pl.when(i == 6 + n)
+            def _():
+                arrive(RELAY_LAST, n)
+
+            @pl.when(i == 4 + n)
+            def _():
+                for k in range(n * FINE // per, (n + 1) * FINE // per):
+                    arrive(RELAY_X, k)
+                send(RELAY_LAST, n)
+
+        grads(1, place, q, pl.multiple_of(j * TILE, TILE), TILE)
+        for n in range(per):
+            @pl.when(i == 2 * n)
+            def _():
+                send(S1_SIB_FAR, n)
+
+            @pl.when(i == 2 * n + 1)
+            def _():
+                send_far(1, n)
+
+            @pl.when(i == 6 + n)
+            def _():
+                send(S1_SIB_OWN, n)
+
+            @pl.when(i == n)
+            def _():
+                for k in range(FINE - 2 + n * 2 // per, FINE - 2 + (n + 1) * 2 // per):
+                    relay(k)
+
+        return carry
+
+    lax.fori_loop(0, 8, second, 0)
+    user_step(1)
     store = pltpu.make_async_copy(users, users_out, out_sem)
     store.start()
-    finish(1, q_c)
+    load_noise_items[1].wait()
+    for k in range(FINE):
+        finish(1, q_c, k)
     for kind in range(KINDS):
         for k in range(count(kind)):
             copy_of(kind, k).wait_send()
@@ -305,6 +321,7 @@
         scratch_shapes=[
             pltpu.SMEM(tile_index.shape, jnp.int32),
             pltpu.SMEM((1, counts.shape[0]), jnp.int32),
+            pltpu.SMEM((2 * (mine // tile) * (items.shape[0] // tile),), jnp.int32),
             pltpu.VMEM(kept, F32),
             pltpu.VMEM((2,) + items.shape, F32),
             pltpu.VMEM((2,) + kept, F32),

time: 36.3 us -> 39.1 us (1.077)
  Pallas kernels: 34.1 us -> 36.9 us
    pallas_call x1, Pallas kernels: 34.1 us -> 36.9 us  [body(): pl.pallas_call(functools.partial(kernel, n_blk), out_shape=(pltpu.VMEM(ke...]
where the time goes in v3:
time: 39.1 us; the launch traced here: 38.9 us
  Pallas kernels  36.9 us (94%)
  local copies, waits for them, and re-layouts  1.41 us (4%)
  between operations  0.64 us (2%)
    pallas_call x1, Pallas kernels, body(): pl.pallas_call(functools.partial(kernel, n_blk), out_shape=(pltpu.VMEM(ke...  36.9 us
    unnamed x2, local copies, waits for them, and re-layouts  1.41 us

profile of v3, /device:TPU:0, one launch (start us, length us, event | category | flops | bytes accessed | tf_op | source)
XLA Modules:
  0.0 38.9 jit_solution(9288186657352243569)
XLA Ops:
  0.6 36.9 %shard_map.95 = (f32[256,256]{1,0:T(8,128)S(1)}, f32[256,256]{1,0:T(8,128)S(1)}) custom-call(s32[2,8]{1,0:T(2,128)} %tiles_hbm.1, s32[1,2]{1,0:T(1,128)} %bitcast.1, f32[256,256]{1,0:T(8,128)} %users_hbm.1, f32[1024,256]{1,0:T(8,128)} %items_hbm.1, f32[2,256,256]{2,1,0:T(8,128)} %noise_users_hbm.1, f32[2,1024,256]{2,1,0:T(8,128)} %noise_items_hbm.1, ...), custom_call_target="tpu_custom_call" | custom-call | flops 2415919104 | bytes 4194304 | tf_op jit(solution)/shard_map/pallas_call | solution.py:316
  37.5 0.7 %copy.12 = f32[256,256]{1,0:T(8,128)} copy(f32[256,256]{1,0:T(8,128)S(1)} %get-tuple-element.2) | data formatting | bytes 524288
  38.2 0.7 %copy.13 = f32[256,256]{1,0:T(8,128)} copy(f32[256,256]{1,0:T(8,128)S(1)} %get-tuple-element.3) | data formatting | bytes 524288

commit v4 on v3

--- a/solution.py
+++ b/solution.py
@@ -46,7 +46,7 @@
 def kernel(n_blk, tiles_hbm, counts_hbm, users_hbm, items_hbm, noise_users_hbm, noise_items_hbm,
            ratings_hbm, weights_hbm, users_out, items_out,
            tiles, counts, table, users, blocks, noise_users, noise_items, ratings, weights,
-           u_wide, u_tall, v_tall, e_wide, part, from_sib_far, from_x,
+           ratings_t, weights_t, ut_tall, u_tall, v_tall, err_t, part, from_sib_far, from_x,
            from_sib_own, moved, local_sem, out_sem, send_sem, recv_sem):
     quarter = users.shape[0]
     per = quarter // TILE
@@ -139,29 +139,34 @@
         slot = table[(stratum * per + row) * item_tiles + column]
         live = jnp.where(slot >= 0, jnp.float32(1), jnp.float32(0))
         slot = jnp.maximum(slot, 0)
-        weight = weights[stratum, slot].astype(F32) * live
-        return weight * (ratings[stratum, slot].astype(F32) - predicted)
+        weight = weights_t[stratum, slot].astype(F32) * live
+        return weight * (ratings_t[stratum, slot].astype(F32) - predicted)
+
+    def turn_tiles(stratum):
+        def turn(i, carry):
+            ratings_t[stratum, i] = ratings[stratum, i].T
+            weights_t[stratum, i] = weights[stratum, i].T
+            return carry
+
+        lax.fori_loop(0, slots, turn, 0)
 
     def grads(stratum, place, q, start, size):
         item_rows = blocks[stratum, rows(q, start, size), :]
-        predicted = dot(u_wide[...], right_triple(item_rows, 1), ((1,), (1,)))
+        predicted = dot(left_triple(item_rows, 1), ut_tall[...], ((1,), (0,)))
         bands = []
-        for r in range(per):
+        for j in range(size // TILE):
+            column = q * per + start // TILE + j
             line = []
-            for j in range(size // TILE):
-                column = q * per + start // TILE + j
+            for r in range(per):
                 line.append(cell_err(stratum, r, column,
-                                     predicted[r * TILE:(r + 1) * TILE, j * TILE:(j + 1) * TILE]))
+                                     predicted[j * TILE:(j + 1) * TILE, r * TILE:(r + 1) * TILE]))
             bands.append(jnp.concatenate(line, axis=1))
         err = jnp.concatenate(bands, axis=0)
-        part[stratum, place, pl.ds(start, size)] = dot(left_triple(err.T, 1), u_tall[...], ((1,), (0,)))
+        part[stratum, place, pl.ds(start, size)] = dot(left_triple(err, 1), u_tall[...], ((1,), (0,)))
+        err_t[place, pl.ds(start, size)] = err
         item_high, item_low = halves(item_rows)
-        err_high, err_low = halves(err)
-        for third, item_part, err_part in ((0, item_high, err_high), (1, item_high, err_low),
-                                           (2, item_low, err_high)):
-            span = pl.ds(pl.multiple_of(third * quarter + start, size), size)
-            v_tall[place, span] = item_part
-            e_wide[place, :, span] = err_part
+        for third, item_part in ((0, item_high), (1, item_high), (2, item_low)):
+            v_tall[place, pl.ds(pl.multiple_of(third * quarter + start, size), size)] = item_part
 
     def send_far(stratum, j):
         span = slice(j * TILE, (j + 1) * TILE)
@@ -173,13 +178,14 @@
 
     def split_users():
         now = users[...]
-        u_wide[...] = left_triple(now, 1)
+        ut_tall[...] = right_triple(now.T, 0)
         u_tall[...] = right_triple(now, 0)
 
     def user_step(stratum):
         now = users[...]
-        total = dot(jnp.concatenate([e_wide[p] for p in range(4)], axis=1),
-                    jnp.concatenate([v_tall[p] for p in range(4)], axis=0), ((1,), (0,)))
+        total = jnp.zeros(now.shape, F32)
+        for p in range(4):
+            total += dot(left_triple(err_t[p].T, 1), v_tall[p], ((1,), (0,)))
         users[...] = now + STEP_SIZE * (LIKELIHOOD * total - now) + NOISE_SCALE * noise_users[stratum]
 
     def item_step(stratum, now, k):
@@ -217,6 +223,7 @@
     split_users()
     load_ratings.wait()
     load_weights.wait()
+    turn_tiles(0)
     pl.semaphore_wait(barrier, 4)
 
     def first(i, carry):
@@ -250,56 +257,64 @@
     split_users()
     for k in range(1, FINE):
         finish(0, q_a, k)
+        if k == 1:
+            turn_tiles(1)
         if k >= 2:
             relay(k - 2)
 
     def second(i, carry):
-        place = jnp.where(i < 4, i % 2, 3 - (i - 4) // 2)
-        j = jnp.where(i < 4, i // 2, i % 2)
-        q = jnp.where(place == 0, q_b, jnp.where(place == 1, q_a, jnp.where(place == 2, q_d, q_c)))
+        place = i % 2
         for n in range(per):
             @pl.when(i == 2 * n)
             def _():
                 arrive(RELAY_SIB, n)
 
-            @pl.when(i == 6 + n)
-            def _():
-                arrive(RELAY_LAST, n)
-
-            @pl.when(i == 4 + n)
-            def _():
+        grads(1, place, jnp.where(place == 0, q_b, q_a), pl.multiple_of(i // 2 * TILE, TILE), TILE)
+        for n in range(per):
+            @pl.when(i == 2 * n)
+            def _():
+                send(S1_SIB_FAR, n)
+
+            @pl.when(i == n)
+            def _():
+                for k in range(FINE - 2 + n * 2 // per, FINE - 2 + (n + 1) * 2 // per):
+                    relay(k)
+
+            @pl.when(i == 2 * n + 1)
+            def _():
+                send_far(1, n)
+
+        return carry
+
+    lax.fori_loop(0, 2 * per, second, 0)
+
+    def third(i, carry):
+        @pl.when(i == 0)
+        def _():
+            for n in range(per):
                 for k in range(n * FINE // per, (n + 1) * FINE // per):
                     arrive(RELAY_X, k)
                 send(RELAY_LAST, n)
 
-        grads(1, place, q, pl.multiple_of(j * TILE, TILE), TILE)
-        for n in range(per):
-            @pl.when(i == 2 * n)
-            def _():
-                send(S1_SIB_FAR, n)
-
-            @pl.when(i == 2 * n + 1)
-            def _():
-                send_far(1, n)
-
-            @pl.when(i == 6 + n)
-            def _():
-                send(S1_SIB_OWN, n)
-
-            @pl.when(i == n)
-            def _():
-                for k in range(FINE - 2 + n * 2 // per, FINE - 2 + (n + 1) * 2 // per):
-                    relay(k)
+        @pl.when(i == 1)
+        def _():
+            arrive_all(RELAY_LAST)
+
+        grads(1, 3 - i, jnp.where(i == 0, q_c, q_d), 0, quarter)
+
+        @pl.when(i == 1)
+        def _():
+            send_all(S1_SIB_OWN)
 
         return carry
 
-    lax.fori_loop(0, 8, second, 0)
+    lax.fori_loop(0, 2, third, 0)
+    load_noise_items[1].wait()
+    for k in range(FINE):
+        finish(1, q_c, k)
     user_step(1)
     store = pltpu.make_async_copy(users, users_out, out_sem)
     store.start()
-    load_noise_items[1].wait()
-    for k in range(FINE):
-        finish(1, q_c, k)
     for kind in range(KINDS):
         for k in range(count(kind)):
             copy_of(kind, k).wait_send()
@@ -328,10 +343,12 @@
             pltpu.VMEM((2,) + kept, F32),
             pltpu.VMEM((2, slots, tile, tile), BF16),
             pltpu.VMEM((2, slots, tile, tile), BF16),
-            pltpu.VMEM((mine, 3 * rank), BF16),
+            pltpu.VMEM((2, slots, tile, tile), BF16),
+            pltpu.VMEM((2, slots, tile, tile), BF16),
+            pltpu.VMEM((3 * rank, mine), BF16),
             pltpu.VMEM((3 * mine, rank), BF16),
             pltpu.VMEM((4, 3 * mine, rank), BF16),
-            pltpu.VMEM((4, mine, 3 * mine), BF16),
+            pltpu.VMEM((4, mine, mine), F32),
             pltpu.VMEM((2, 4) + kept, F32),
             pltpu.VMEM((2,) + kept, F32),
             pltpu.VMEM((2,) + kept, F32),

time: 39.1 us -> 39.4 us (level)
  no operation moved by 1% of the time
where the time goes in v4:
time: 39.4 us; the launch traced here: 39.2 us
  Pallas kernels  37.2 us (94%)
  local copies, waits for them, and re-layouts  1.41 us (4%)
  between operations  0.64 us (2%)
    pallas_call x1, Pallas kernels, body(): pl.pallas_call(functools.partial(kernel, n_blk), out_shape=(pltpu.VMEM(ke...  37.2 us
    unnamed x2, local copies, waits for them, and re-layouts  1.41 us

profile of v4, /device:TPU:0, one launch (start us, length us, event | category | flops | bytes accessed | tf_op | source)
XLA Modules:
  0.0 39.2 jit_solution(8988576481052830781)
XLA Ops:
  0.6 37.2 %shard_map.95 = (f32[256,256]{1,0:T(8,128)S(1)}, f32[256,256]{1,0:T(8,128)S(1)}) custom-call(s32[2,8]{1,0:T(2,128)} %tiles_hbm.1, s32[1,2]{1,0:T(1,128)} %bitcast.1, f32[256,256]{1,0:T(8,128)} %users_hbm.1, f32[1024,256]{1,0:T(8,128)} %items_hbm.1, f32[2,256,256]{2,1,0:T(8,128)} %noise_users_hbm.1, f32[2,1024,256]{2,1,0:T(8,128)} %noise_items_hbm.1, ...), custom_call_target="tpu_custom_call" | custom-call | flops 2415919104 | bytes 4194304 | tf_op jit(solution)/shard_map/pallas_call | solution.py:331
  37.8 0.7 %copy.12 = f32[256,256]{1,0:T(8,128)} copy(f32[256,256]{1,0:T(8,128)S(1)} %get-tuple-element.2) | data formatting | bytes 524288
  38.5 0.7 %copy.13 = f32[256,256]{1,0:T(8,128)} copy(f32[256,256]{1,0:T(8,128)S(1)} %get-tuple-element.3) | data formatting | bytes 524288

commit v5 on v3

--- a/solution.py
+++ b/solution.py
@@ -45,7 +45,7 @@
 
 def kernel(n_blk, tiles_hbm, counts_hbm, users_hbm, items_hbm, noise_users_hbm, noise_items_hbm,
            ratings_hbm, weights_hbm, users_out, items_out,
-           tiles, counts, table, users, blocks, noise_users, noise_items, ratings, weights,
+           tiles, counts, table, users, blocks, noise_users, noise_items, ratings0, weights0, ratings1, weights1,
            u_wide, u_tall, v_tall, e_wide, part, from_sib_far, from_x,
            from_sib_own, moved, local_sem, out_sem, send_sem, recv_sem):
     quarter = users.shape[0]
@@ -85,8 +85,8 @@
     load_counts = load(1, counts_hbm, counts)
     load_users = load(2, users_hbm, users)
     load_items = [load(3, items_hbm.at[rows(q_d)], items.at[rows(q_d)])]
-    load_ratings = load(4, ratings_hbm, ratings)
-    load_weights = load(5, weights_hbm, weights)
+    load_ratings = [load(4, ratings_hbm.at[0], ratings0)]
+    load_weights = [load(5, weights_hbm.at[0], weights0)]
     barrier = pltpu.get_barrier_semaphore()
     for other in (sibling, across, ahead, behind):
         pl.semaphore_signal(barrier, inc=1, device_id=other, device_id_type=MESH)
@@ -95,6 +95,9 @@
     load_noise_users = load(9, noise_users_hbm, noise_users)
     load_noise_items = [load(10, noise_items_hbm.at[0, rows(q_a)], noise_items.at[0]),
                         load(11, noise_items_hbm.at[1, rows(q_c)], noise_items.at[1])]
+
+    load_ratings.append(load(12, ratings_hbm.at[1], ratings1))
+    load_weights.append(load(13, weights_hbm.at[1], weights1))
 
     def remote(kind, k, source, target, device):
         return pltpu.make_async_remote_copy(
@@ -139,8 +142,8 @@
         slot = table[(stratum * per + row) * item_tiles + column]
         live = jnp.where(slot >= 0, jnp.float32(1), jnp.float32(0))
         slot = jnp.maximum(slot, 0)
-        weight = weights[stratum, slot].astype(F32) * live
-        return weight * (ratings[stratum, slot].astype(F32) - predicted)
+        ratings, weights = ((ratings0, weights0), (ratings1, weights1))[stratum]
+        return weights[slot].astype(F32) * live * (ratings[slot].astype(F32) - predicted)
 
     def grads(stratum, place, q, start, size):
         item_rows = blocks[stratum, rows(q, start, size), :]
@@ -215,8 +218,8 @@
     lax.fori_loop(0, 2 * per * item_tiles, fill_table, 0)
     load_users.wait()
     split_users()
-    load_ratings.wait()
-    load_weights.wait()
+    load_ratings[0].wait()
+    load_weights[0].wait()
     pl.semaphore_wait(barrier, 4)
 
     def first(i, carry):
@@ -253,53 +256,53 @@
         if k >= 2:
             relay(k - 2)
 
+    for k in range(FINE - 2, FINE):
+        relay(k)
+    load_ratings[1].wait()
+    load_weights[1].wait()
+    load_noise_items[1].wait()
+
     def second(i, carry):
-        place = jnp.where(i < 4, i % 2, 3 - (i - 4) // 2)
-        j = jnp.where(i < 4, i // 2, i % 2)
-        q = jnp.where(place == 0, q_b, jnp.where(place == 1, q_a, jnp.where(place == 2, q_d, q_c)))
-        for n in range(per):
-            @pl.when(i == 2 * n)
-            def _():
-                arrive(RELAY_SIB, n)
-
-            @pl.when(i == 6 + n)
-            def _():
-                arrive(RELAY_LAST, n)
-
-            @pl.when(i == 4 + n)
-            def _():
+        @pl.when(i == 0)
+        def _():
+            arrive_all(RELAY_SIB)
+
+        @pl.when(i == 2)
+        def _():
+            for n in range(per):
                 for k in range(n * FINE // per, (n + 1) * FINE // per):
                     arrive(RELAY_X, k)
                 send(RELAY_LAST, n)
 
-        grads(1, place, q, pl.multiple_of(j * TILE, TILE), TILE)
-        for n in range(per):
-            @pl.when(i == 2 * n)
-            def _():
-                send(S1_SIB_FAR, n)
-
-            @pl.when(i == 2 * n + 1)
-            def _():
+        @pl.when(i == 3)
+        def _():
+            arrive_all(RELAY_LAST)
+
+        place = jnp.where(i < 2, i, 5 - i)
+        q = jnp.where(i == 0, q_b, jnp.where(i == 1, q_a, jnp.where(i == 2, q_c, q_d)))
+        grads(1, place, q, 0, quarter)
+
+        @pl.when(i == 0)
+        def _():
+            send_all(S1_SIB_FAR)
+
+        @pl.when(i == 1)
+        def _():
+            for n in range(per):
                 send_far(1, n)
 
-            @pl.when(i == 6 + n)
-            def _():
-                send(S1_SIB_OWN, n)
-
-            @pl.when(i == n)
-            def _():
-                for k in range(FINE - 2 + n * 2 // per, FINE - 2 + (n + 1) * 2 // per):
-                    relay(k)
+        @pl.when(i == 3)
+        def _():
+            send_all(S1_SIB_OWN)
 
         return carry
 
-    lax.fori_loop(0, 8, second, 0)
+    lax.fori_loop(0, 4, second, 0)
+    for k in range(FINE):
+        finish(1, q_c, k)
     user_step(1)
     store = pltpu.make_async_copy(users, users_out, out_sem)
     store.start()
-    load_noise_items[1].wait()
-    for k in range(FINE):
-        finish(1, q_c, k)
     for kind in range(KINDS):
         for k in range(count(kind)):
             copy_of(kind, k).wait_send()
@@ -326,8 +329,10 @@
             pltpu.VMEM((2,) + items.shape, F32),
             pltpu.VMEM((2,) + kept, F32),
             pltpu.VMEM((2,) + kept, F32),
-            pltpu.VMEM((2, slots, tile, tile), BF16),
-            pltpu.VMEM((2, slots, tile, tile), BF16),
+            pltpu.VMEM((slots, tile, tile), BF16),
+            pltpu.VMEM((slots, tile, tile), BF16),
+            pltpu.VMEM((slots, tile, tile), BF16),
+            pltpu.VMEM((slots, tile, tile), BF16),
             pltpu.VMEM((mine, 3 * rank), BF16),
             pltpu.VMEM((3 * mine, rank), BF16),
             pltpu.VMEM((4, 3 * mine, rank), BF16),
@@ -337,7 +342,7 @@
             pltpu.VMEM((2,) + kept, F32),
             pltpu.VMEM((2,) + kept, F32),
             pltpu.VMEM((2,) + kept, F32),
-            pltpu.SemaphoreType.DMA((12,)),
+            pltpu.SemaphoreType.DMA((14,)),
             pltpu.SemaphoreType.DMA,
             pltpu.SemaphoreType.DMA((KINDS, FINE)),
             pltpu.SemaphoreType.DMA((KINDS, FINE)),

time: 39.1 us -> 36.2 us (0.926)
  Pallas kernels: 36.9 us -> 34 us
    pallas_call x1, Pallas kernels: 36.9 us -> 34 us  [body(): pl.pallas_call(functools.partial(kernel, n_blk), out_shape=(pltpu.VMEM(ke...]
where the time goes in v5:
time: 36.2 us; the launch traced here: 36 us
  Pallas kernels  34 us (94%)
  local copies, waits for them, and re-layouts  1.41 us (4%)
  between operations  0.64 us (2%)
    pallas_call x1, Pallas kernels, body(): pl.pallas_call(functools.partial(kernel, n_blk), out_shape=(pltpu.VMEM(ke...  34 us
    unnamed x2, local copies, waits for them, and re-layouts  1.41 us

profile of v5, /device:TPU:0, one launch (start us, length us, event | category | flops | bytes accessed | tf_op | source)
XLA Modules:
  0.0 36.0 jit_solution(12606064887375286292)
XLA Ops:
  0.6 34.0 %shard_map.95 = (f32[256,256]{1,0:T(8,128)S(1)}, f32[256,256]{1,0:T(8,128)S(1)}) custom-call(s32[2,8]{1,0:T(2,128)} %tiles_hbm.1, s32[1,2]{1,0:T(1,128)} %bitcast.1, f32[256,256]{1,0:T(8,128)} %users_hbm.1, f32[1024,256]{1,0:T(8,128)} %items_hbm.1, f32[2,256,256]{2,1,0:T(8,128)} %noise_users_hbm.1, f32[2,1024,256]{2,1,0:T(8,128)} %noise_items_hbm.1, ...), custom_call_target="tpu_custom_call" | custom-call | flops 2415919104 | bytes 4194304 | tf_op jit(solution)/shard_map/pallas_call | solution.py:319
  34.6 0.7 %copy.12 = f32[256,256]{1,0:T(8,128)} copy(f32[256,256]{1,0:T(8,128)S(1)} %get-tuple-element.2) | data formatting | bytes 524288
  35.3 0.7 %copy.13 = f32[256,256]{1,0:T(8,128)} copy(f32[256,256]{1,0:T(8,128)S(1)} %get-tuple-element.3) | data formatting | bytes 524288

commit v6 on v5

--- a/solution.py
+++ b/solution.py
@@ -12,7 +12,8 @@
 LIKELIHOOD = 20.0
 NOISE_SCALE = math.sqrt(0.002)
 TILE = 128
-FINE = 4
+FINE = 8
+LAG = FINE // 2
 MESH = pl.DeviceIdType.MESH
 F32 = jnp.float32
 BF16 = jnp.bfloat16
@@ -253,10 +254,10 @@
     split_users()
     for k in range(1, FINE):
         finish(0, q_a, k)
-        if k >= 2:
-            relay(k - 2)
-
-    for k in range(FINE - 2, FINE):
+        if k >= LAG:
+            relay(k - LAG)
+
+    for k in range(FINE - LAG, FINE):
         relay(k)
     load_ratings[1].wait()
     load_weights[1].wait()

time: 36.2 us -> 36.7 us (1.014)
  Pallas kernels: 34 us -> 34.5 us
    pallas_call x1, Pallas kernels: 34 us -> 34.5 us  [body(): pl.pallas_call(functools.partial(kernel, n_blk), out_shape=(pltpu.VMEM(ke...]
where the time goes in v6:
time: 36.7 us; the launch traced here: 36.5 us
  Pallas kernels  34.5 us (94%)
  local copies, waits for them, and re-layouts  1.41 us (4%)
  between operations  0.64 us (2%)
    pallas_call x1, Pallas kernels, body(): pl.pallas_call(functools.partial(kernel, n_blk), out_shape=(pltpu.VMEM(ke...  34.5 us
    unnamed x2, local copies, waits for them, and re-layouts  1.41 us

profile of v6, /device:TPU:0, one launch (start us, length us, event | category | flops | bytes accessed | tf_op | source)
XLA Modules:
  0.0 36.5 jit_solution(13294163136681827238)
XLA Ops:
  0.6 34.5 %shard_map.95 = (f32[256,256]{1,0:T(8,128)S(1)}, f32[256,256]{1,0:T(8,128)S(1)}) custom-call(s32[2,8]{1,0:T(2,128)} %tiles_hbm.1, s32[1,2]{1,0:T(1,128)} %bitcast.1, f32[256,256]{1,0:T(8,128)} %users_hbm.1, f32[1024,256]{1,0:T(8,128)} %items_hbm.1, f32[2,256,256]{2,1,0:T(8,128)} %noise_users_hbm.1, f32[2,1024,256]{2,1,0:T(8,128)} %noise_items_hbm.1, ...), custom_call_target="tpu_custom_call" | custom-call | flops 2415919104 | bytes 4194304 | tf_op jit(solution)/shard_map/pallas_call | solution.py:320
  35.1 0.7 %copy.12 = f32[256,256]{1,0:T(8,128)} copy(f32[256,256]{1,0:T(8,128)S(1)} %get-tuple-element.2) | data formatting | bytes 524288
  35.8 0.7 %copy.13 = f32[256,256]{1,0:T(8,128)} copy(f32[256,256]{1,0:T(8,128)S(1)} %get-tuple-element.3) | data formatting | bytes 524288
